TPU v7x, 512 devices: a whole 4x8x8 slice. The times are simulated.
512 devices in a mesh: tm: 16 (over x, z_hi, core), cell: 32 (over y, z_lo).
Axes of the slice: x: 4, y: 8, z: 8 (z_hi: 2, z_lo: 4; z = z_hi * 4 + z_lo), core: 2. Of those that a mesh axis runs over, the one named last changes fastest.
Arguments:
- sensitivity: bfloat16 [2048, 16, 16384], P(None, 'tm', 'cell'), may hold values from -0.25 to 0.25
- duals: bfloat16 [2048, 128], P(('tm', 'cell')), may hold values from -6 to 6
- time_cov: float32 [16, 16], replicated, may hold values from 0.05 to 0.5
- cell_coords: int32 [2, 16384], P(None, 'cell'), may hold values from 0 to 127, as said below
- obs_time: int32 [2048], replicated, may hold values from 0 to 15
- obs_owner: int32 [2048], replicated, may hold values from 0 to 2047, each once
Outputs:
- product: float32 [2048, 128], P(('tm', 'cell'))
Inputs may be any that keep to these rules, and one draw needn't show every extreme that they name: `cell_coords`: every cell has its own grid position; rows lie below 128 and columns below 128. `obs_owner`: every observation stands in exactly one slot.
All inputs are finite; a program needn't handle non-finite values.
Results may differ from a plain program's by a relative error of at most 0.0049.
Values may be sent and summed in bfloat16 or wider, within the bound.
No kernel may reach another device: no remote copies, remote signals or barrier semaphores. Data moves between devices by JAX's collectives and lax.ppermute only.
A program may use at most 64 MiB of HBM per device.

v0:
```python
import jax
import jax.numpy as jnp
from jax import lax
from jax.sharding import Mesh
from jax.sharding import PartitionSpec as P

LSCALE = 4
TM = ("tm_0", "tm_1", "tm_2")
TM_CELL = ("tm_0", "tm_1", "tm_2", "cell_0", "cell_1")
CELL = ("cell_0", "cell_1")


def laid_out(pieces, dim):
    pieces = jnp.moveaxis(pieces, 0, dim)
    shape = pieces.shape
    return pieces.reshape(*shape[:dim], shape[dim] * shape[dim + 1], *shape[dim + 2 :])


def sent_to_all(array, axis):
    copies = jnp.broadcast_to(array, (lax.axis_size(axis), *array.shape))
    return lax.all_to_all(copies, axis, split_axis=0, concat_axis=0, tiled=True)


def gathered_copies(array, axis, dim):
    return laid_out(sent_to_all(array, axis), dim)


def cut_along(array, dim, length):
    shape = array.shape
    pieces = array.reshape(*shape[:dim], length, shape[dim] // length, *shape[dim + 1 :])
    return jnp.moveaxis(pieces, dim, 0)


def edges_of(length, count):
    hop = length // count
    if hop >= 8:
        hop -= hop % 8
    return [hop * k for k in range(1, count)]


def own_block(pieces, axes, sequence):
    inside = pieces.shape[1:]
    pieces = pieces.reshape(*(lax.axis_size(a) for a in axes), *inside)
    pieces = jnp.moveaxis(pieces, sequence, range(len(axes))).reshape(-1, *inside)
    for k in sequence:
        pieces = lax.psum_scatter(pieces, axes[k], scatter_dimension=0, tiled=True)
    return pieces[0]


def sum_at_once(array, axes, dim):
    pieces = cut_along(array, dim, lax.axis_size(axes))
    widest = max(range(1, max(2, pieces.ndim - 1)), key=lambda d: pieces.shape[d])
    count, done = (len(axes), [])
    for first, slab in enumerate(
        jnp.split(pieces, edges_of(pieces.shape[widest], count), axis=widest)
    ):
        if slab.size:
            sequence = [(first + k) % count for k in range(count)]
            done.append(own_block(slab, axes, sequence))
    return jnp.concatenate(done, axis=widest - 1)


def covariance(left_coords, right_coords):
    row_gap = (left_coords[0][:, None] - right_coords[0][None, :]).astype(jnp.float32)
    col_gap = (left_coords[1][:, None] - right_coords[1][None, :]).astype(jnp.float32)
    distance = jnp.sqrt(row_gap * row_gap + col_gap * col_gap)
    return (jnp.exp(-distance / LSCALE) / (8.0 * LSCALE)).astype(jnp.bfloat16)


def per_device(sensitivity, duals, time_cov, cell_coords, obs_time, obs_owner):
    obs_count = sensitivity.shape[0]
    time_count = sensitivity.shape[1]
    cell_count = sensitivity.shape[2]
    real_count = duals.shape[1]
    first_time = lax.axis_index(TM) * time_count
    time_index = first_time + jnp.arange(time_count, dtype=jnp.int32)
    live = time_index[None, :, None] <= obs_time[:, None, None]
    masked = jnp.where(live, sensitivity, jnp.zeros((), jnp.bfloat16))
    flattened = masked.reshape(obs_count, time_count * cell_count)
    picked = flattened
    adjoint = lax.dot_general(
        picked,
        lax.all_gather(duals, TM_CELL, axis=0, tiled=True),
        (((0,), (0,)), ((), ())),
        preferred_element_type=jnp.float32,
    )
    local_adj = (
        adjoint.astype(jnp.bfloat16).reshape(time_count, cell_count, real_count).transpose(1, 0, 2)
    )
    all_coords = gathered_copies(cell_coords, CELL, 1)
    spread_adj = lax.all_to_all(local_adj, TM, split_axis=2, concat_axis=1, tiled=True)
    values = jnp.einsum(
        "st,ctr->csr", time_cov, spread_adj.astype(jnp.float32), precision=lax.Precision.HIGHEST
    ).astype(jnp.bfloat16)
    portion = lax.all_gather(values, CELL, axis=0, tiled=True)
    kernel = covariance(cell_coords, all_coords)
    summed = jnp.dot(
        kernel, portion.reshape(portion.shape[0], -1), preferred_element_type=jnp.float32
    )
    weighted = lax.all_to_all(
        summed.reshape(values.shape).astype(jnp.bfloat16),
        TM,
        split_axis=1,
        concat_axis=2,
        tiled=True,
    )
    weighted_flat = weighted.transpose(1, 0, 2).reshape(time_count * cell_count, real_count)
    picked = jnp.take(flattened, obs_owner, axis=0)
    return sum_at_once(
        jnp.dot(picked, weighted_flat, preferred_element_type=jnp.float32), TM_CELL, 0
    )


def solution(mesh):
    split = Mesh(mesh.devices.reshape(4, 2, 2, 8, 4), ("tm_0", "tm_1", "tm_2", "cell_0", "cell_1"))
    return jax.shard_map(
        per_device,
        mesh=split,
        in_specs=(P(None, TM, CELL), P(TM_CELL, None), P(), P(None, CELL), P(), P()),
        out_specs=P(TM_CELL, None),
        check_vma=False,
    )
```

profile of v0, /device:TPU:2, one launch (start us, length us, event | category | flops | bytes accessed | tf_op | source)
XLA Modules:
  0.0 1611.9 jit_solution(16433688849147574105)
XLA Ops:
  6.5 0.0 copy-start
  6.5 0.0 all-gather.3.cloned.1.call-start
  6.5 1138.5 %all-gather = bf16[512,4,128]{2,1,0:T(4,128)(2,1)S(1)} all-gather(bf16[1,4,128]{2,1,0:T(4,128)(2,1)} %bitcast.57), channel_id=1, replica_groups=mesh['tm_0'=4,'tm_1'=2,'tm_2'=2,'cell_0'=8,'cell_1'=4] {'tm_0','tm_1','t..., dimensions={0}, use_global_device_ids=true | all-gather | bytes 525312 | tf_op jit(solution)/shard_map/all_gather | solution.py:83
  1145.0 0.7 broadcast_compare_fusion
  1145.7 0.0 copy-start.3
  1145.7 0.0 copy-start.2
  1145.7 1.8 select_bitcast_fusion
  1147.5 0.8 fusion.14
  1148.3 0.2 copy.17
  1148.5 0.5 broadcast.41
  1149.0 1.4 reduce
  1150.4 0.1 reshape.87
  1150.5 126.0 %all_to_all.26 = bf16[16,2,2048]{2,1,0:T(2,128)(2,1)S(1)} all-to-all(bf16[16,2,2048]{2,1,0:T(2,128)(2,1)S(1)} %reshape.87), channel_id=1, replica_groups=mesh['tm_0'=4,'tm_1'=2,'tm_2'=2,'cell_0'=8,'cell_1'=4] {'tm_0','tm_1','t..., dimensions={0} | all-to-all | bytes 262144 | tf_op jit(solution)/shard_map/all_to_all | solution.py:91
  1276.5 0.1 reshape.88
  1276.6 0.0 copy-done
  1276.7 0.9 fusion.15
  1277.6 0.0 all-gather.3.cloned.1.call-update
  1277.6 0.0 copy-done.3
  1277.6 0.7 broadcast_in_dim.33
  1278.3 3.9 all-to-all-start
  1282.2 0.0 copy-done.2
  1282.2 9.2 gather_fusion
  1291.4 3.9 all-to-all-done
  1295.3 0.1 fusion.22
  1295.4 136.2 %all-gather.3.cloned.1.call-done = bf16[16384,16,8]{0,1,2:T(8,128)(2,1)} async-done(((bf16[512,16,8]{0,1,2:T(8,128)(2,1)}), bf16[16384,16,8]{0,1,2:T(8,128)(2,1)}) %all-gather.3.cloned.1.call-update) | async-done | bytes 4194320 | tf_op jit(solution)/shard_map/all_gather | solution.py:95
  1431.6 0.0 copy-start.1
  1431.6 22.9 %fusion.9 = bf16[512,16,8]{0,1,2:T(8,128)(2,1)S(1)} fusion(bf16[16384,16,8]{0,1,2:T(8,128)(2,1)} %all-gather.3.cloned.1.call-done, s32[16384]{0:T(1024)S(1)} %bitcast.54, s32[512]{0:T(512)S(1)} %bitcast.56, s32[16384]{0:T(1024)S(1)} %bitcast.53, s32[512]{0:T(512)S(1)} %bitcast.55), kind=kOutput, calls=%fused_computation.12 | convolution fusion | flops 2239823872 | bytes 4460544 | tf_op jit(solution)/shard_map/dot_general | solution.py:97
  1454.5 0.7 copy.21
  1455.3 7.0 all-to-all-start.2
  1462.2 0.0 reduce-scatter.5.cloned.1.call-start
  1462.3 0.0 copy-done.1
  1462.3 1.6 broadcast_select_fusion
  1463.9 2.5 select_n.30
  1466.4 4.6 all-to-all-done.2
  1471.0 1.3 fusion.6
  1472.3 1.1 copy.24
  1473.5 0.0 reduce-scatter.5.cloned.1.call-update
  1473.5 0.0 reduce-scatter.7.cloned.1.call-start
  1473.5 32.9 %reduce-scatter.5.cloned.1.call-done = f32[128,4,128]{2,0,1:T(8,128)} async-done(((f32[512,4,128]{2,0,1:T(8,128)}), f32[128,4,128]{2,0,1:T(8,128)}) %reduce-scatter.5.cloned.1.call-update) | async-done | bytes 262160 | tf_op jit(solution)/shard_map/reduce_scatter | solution.py:46
  1506.4 0.0 reduce-scatter.7.cloned.1.call-update
  1506.5 0.0 reduce-scatter.9.cloned.1.call-start
  1506.5 26.7 %reduce-scatter.7.cloned.1.call-done = f32[32,4,128]{2,0,1:T(8,128)} async-done(((f32[128,4,128]{2,0,1:T(8,128)}), f32[32,4,128]{2,0,1:T(8,128)}) %reduce-scatter.7.cloned.1.call-update) | async-done | bytes 65552 | tf_op jit(solution)/shard_map/reduce_scatter | solution.py:46
  1533.2 0.0 reduce-scatter.9.cloned.1.call-update
  1533.2 0.0 reduce-scatter.11.cloned.1.call-start
  1533.2 26.2 %reduce-scatter.9.cloned.1.call-done = f32[16,4,128]{2,0,1:T(8,128)} async-done(((f32[32,4,128]{2,0,1:T(8,128)}), f32[16,4,128]{2,0,1:T(8,128)}) %reduce-scatter.9.cloned.1.call-update) | async-done | bytes 32784 | tf_op jit(solution)/shard_map/reduce_scatter | solution.py:46
  1559.4 0.0 reduce-scatter.11.cloned.1.call-update
  1559.4 1.3 dynamic-slice
  1560.8 12.9 reduce-scatter.11.cloned.1.call-done
  1573.7 0.7 copy.25
  1574.4 29.7 %all-reduce = f32[8,4,128]{2,1,0:T(4,128)S(1)} all-reduce(f32[8,4,128]{2,1,0:T(4,128)S(1)} %copy.25), channel_id=6, replica_groups=mesh['tm_0'=4,'tm_1'=2,'tm_2'=2,'cell_0'=8,'cell_1'=4] {'cell_0'}, use_global_device_ids=true, to_apply=%region_4.5.clone | all-reduce | flops 4096 | bytes 32768
  1604.1 1.3 dynamic-slice_bitcast_fusion
  (4 shorter events, 0.0 us)
Async XLA Ops:
  6.5 1270.1 %copy-start = (f32[16,16]{1,0:T(8,128)S(1)}, f32[16,16]{1,0:T(8,128)}, u32[]{:S(2)}) copy-start(f32[16,16]{1,0:T(8,128)} %param.8) | copy-start | bytes 3076
  6.5 1425.1 %all-gather.3.cloned.1.call-start = ((), (), s32[]{:S(2)}) async-start(), calls=%async_computation.7 | async-start | bytes 4325376 | tf_op jit(solution)/shard_map/all_gather | solution.py:95
  1145.7 131.9 %copy-start.3 = (s32[2,512]{1,0:T(2,128)S(1)}, s32[2,512]{1,0:T(2,128)}, u32[]{:S(2)}) copy-start(s32[2,512]{1,0:T(2,128)} %param.9) | copy-start | bytes 12292
  1145.7 136.4 %copy-start.2 = (s32[2048]{0:T(1024)S(1)}, s32[2048]{0:T(1024)}, u32[]{:S(2)}) copy-start(s32[2048]{0:T(1024)} %param.11) | copy-start | bytes 24580
  1278.3 17.0 %all-to-all-start = ((s32[32,2,512]{2,1,0:T(2,128)}), s32[32,2,512]{2,1,0:T(2,128)S(1)}, u32[]{:S(2)}, u32[]{:S(2)}) async-start(s32[32,2,512]{2,1,0:T(2,128)} %broadcast_in_dim.33), calls=%async_computation | async-start | bytes 262144 | tf_op jit(solution)/shard_map/all_to_all | solution.py:21
  1431.6 30.7 %copy-start.1 = (bf16[2048,512]{1,0:T(8,128)(2,1)S(1)}, bf16[2048,512]{1,0:T(8,128)(2,1)}, u32[]{:S(2)}) copy-start(bf16[2048,512]{1,0:T(8,128)(2,1)} %gather_fusion) | copy-start | bytes 6291460
  1455.3 15.8 all-to-all-start.2
  1462.2 44.2 %reduce-scatter.5.cloned.1.call-start = ((), (), s32[]{:S(2)}) async-start(), calls=%async_computation.8 | async-start | bytes 1310720 | tf_op jit(solution)/shard_map/reduce_scatter | solution.py:46
  1473.5 59.7 %reduce-scatter.7.cloned.1.call-start = ((), (), s32[]{:S(2)}) async-start(), calls=%async_computation.9 | async-start | bytes 327680 | tf_op jit(solution)/shard_map/reduce_scatter | solution.py:46
  1506.5 52.9 %reduce-scatter.9.cloned.1.call-start = ((), (), s32[]{:S(2)}) async-start(), calls=%async_computation.10 | async-start | bytes 98304 | tf_op jit(solution)/shard_map/reduce_scatter | solution.py:46
  1533.2 40.5 %reduce-scatter.11.cloned.1.call-start = ((), (), s32[]{:S(2)}) async-start(), calls=%async_computation.11 | async-start | bytes 49152 | tf_op jit(solution)/shard_map/reduce_scatter | solution.py:46
Sparse Core Ops, SparseCore 0:
  1277.7 153.8 all-gather.2
  1473.6 32.7 reduce-scatter.4
  1509.5 23.6 reduce-scatter.6
  1535.8 23.5 reduce-scatter.8
  1562.0 11.6 reduce-scatter.10
where the time goes:
time: 1610 us
  blocking collectives  1290 us (80%)
  waiting for transfers between devices  243 us (15%)
  matrix products  25.9 us (2%)
  local copies, waits for them, and re-layouts  18.6 us (1%)
    all_gather x1, blocking collectives, per_device(): lax.all_gather(duals, TM_CELL, axis=0, tiled=True)  1140 us
    all_gather x1, waiting for transfers between devices, per_device(): portion = lax.all_gather(values, CELL, axis=0, tiled=True)  136 us
    all_to_all x1, blocking collectives, per_device(): lax.all_to_all(local_adj, TM, split_axis=2, concat_axis=1, tiled=True)  126 us
    reduce_scatter x4, waiting for transfers between devices, own_block(): pieces = lax.psum_scatter(pieces, axes[k], scatter_dimension=0, tiled=True)  98.7 us
  transfers between devices with their start and end apart: 7, of which 7 were waited for; matrix products, arithmetic and copies ran while one was open for 1% of the time, Pallas kernels for 0%

commit v1 on v0

--- a/solution.py
+++ b/solution.py
@@ -80,7 +80,9 @@
     picked = flattened
     adjoint = lax.dot_general(
         picked,
-        lax.all_gather(duals, TM_CELL, axis=0, tiled=True),
+        jnp.concatenate(
+            lax.all_to_all(jnp.stack([duals] * lax.axis_size(TM_CELL)), TM_CELL, 0, 0), axis=0
+        ),
         (((0,), (0,)), ((), ())),
         preferred_element_type=jnp.float32,
     )

time: 1610 us -> 405 us (0.25)
  blocking collectives: 1290 us -> 43.6 us
  waiting for transfers between devices: 243 us -> 264 us
  starting transfers between devices: 11 us -> 31.9 us
    all_gather x1 -> x0, blocking collectives: 1140 us -> none  [per_device(): lax.all_gather(duals, TM_CELL, axis=0, tiled=True)]
    all_to_all x1, blocking collectives: 126 us -> 13.9 us  [per_device(): lax.all_to_all(local_adj, TM, split_axis=2, concat_axis=1, tiled=True)]
    all_to_all x0 -> x1, starting transfers between devices: none -> 21.2 us  [per_device(): lax.all_to_all(jnp.stack([duals] * lax.axis_size(TM_CELL)), TM_CELL, 0, 0)]
    all_to_all x0 -> x1, waiting for transfers between devices: none -> 19.2 us  [per_device(): lax.all_to_all(jnp.stack([duals] * lax.axis_size(TM_CELL)), TM_CELL, 0, 0)]
  transfers between devices with their start and end apart: 7 -> 8, of which waited for: 7 -> 8; matrix products, arithmetic and copies ran while one was open for 1% -> 4% of each run, Pallas kernels for 0% -> 0%
where the time goes in v1:
time: 405 us; the launch traced here: 404 us
  waiting for transfers between devices  264 us (65%)
  blocking collectives  43.6 us (11%)
  starting transfers between devices  31.9 us (8%)
  matrix products  25.9 us (6%)
  local copies, waits for them, and re-layouts  20.1 us (5%)
  between operations  13.3 us (3%)
  other arithmetic  5.5 us (1%)
    all_gather x1, waiting for transfers between devices, per_device(): portion = lax.all_gather(values, CELL, axis=0, tiled=True)  138 us
    reduce_scatter x4, waiting for transfers between devices, own_block(): pieces = lax.psum_scatter(pieces, axes[k], scatter_dimension=0, tiled=True)  98.7 us
    unnamed x1, blocking collectives  29.7 us
    dot_general x1, matrix products, per_device(): jnp.dot(kernel, portion.reshape(portion.shape[0], -1), preferred_element_...  22.9 us
    all_to_all x1, starting transfers between devices, per_device(): lax.all_to_all(jnp.stack([duals] * lax.axis_size(TM_CELL)), TM_CELL, 0, 0)  21.2 us
    all_to_all x1, waiting for transfers between devices, per_device(): lax.all_to_all(jnp.stack([duals] * lax.axis_size(TM_CELL)), TM_CELL, 0, 0)  19.2 us
    all_to_all x1, blocking collectives, per_device(): lax.all_to_all(local_adj, TM, split_axis=2, concat_axis=1, tiled=True)  13.9 us
    gather x1, local copies, waits for them, and re-layouts, per_device(): picked = jnp.take(flattened, obs_owner, axis=0)  9.19 us
  transfers between devices with their start and end apart: 8, of which 8 were waited for; matrix products, arithmetic and copies ran while one was open for 4% of the time, Pallas kernels for 0%

profile of v1, /device:TPU:2, one launch (start us, length us, event | category | flops | bytes accessed | tf_op | source)
XLA Modules:
  0.0 404.2 jit_solution(6892822780598385411)
XLA Ops:
  6.5 0.0 copy-start
  6.5 1.6 stack.2
  8.2 21.2 %all-to-all-start.1 = ((bf16[512,4,128]{2,1,0:T(4,128)(2,1)}), bf16[512,4,128]{2,1,0:T(4,128)(2,1)S(1)}, u32[]{:S(2)}, u32[]{:S(2)}) async-start(bf16[512,4,128]{2,1,0:T(4,128)(2,1)} %stack.2), calls=%async_computation.1 | async-start | bytes 1048576 | tf_op jit(solution)/shard_map/all_to_all | solution.py:84
  29.4 0.0 all-gather.2.cloned.1.call-start
  29.4 0.7 broadcast_compare_fusion
  30.1 0.0 copy-start.3
  30.1 0.0 copy-start.2
  30.1 1.8 select_bitcast_fusion
  31.9 19.2 %all-to-all-done.1 = bf16[512,4,128]{2,1,0:T(4,128)(2,1)S(1)} async-done(((bf16[512,4,128]{2,1,0:T(4,128)(2,1)}), bf16[512,4,128]{2,1,0:T(4,128)(2,1)S(1)}, u32[]{:S(2)}, u32[]{:S(2)}) %all-to-all-start.1) | async-done | bytes 524320 | tf_op jit(solution)/shard_map/all_to_all | solution.py:84
  51.1 0.8 fusion.14
  51.9 0.2 copy.17
  52.1 0.5 broadcast.43
  52.6 1.4 reduce
  54.0 0.1 reshape.91
  54.1 13.9 %all_to_all.31 = bf16[16,2,2048]{2,1,0:T(2,128)(2,1)S(1)} all-to-all(bf16[16,2,2048]{2,1,0:T(2,128)(2,1)S(1)} %reshape.91), channel_id=1, replica_groups=mesh['tm_0'=4,'tm_1'=2,'tm_2'=2,'cell_0'=8,'cell_1'=4] {'tm_0','tm_1','t..., dimensions={0} | all-to-all | bytes 262144 | tf_op jit(solution)/shard_map/all_to_all | solution.py:93
  67.9 0.1 reshape.92
  68.1 0.0 copy-done
  68.1 0.9 fusion.15
  69.0 0.0 all-gather.2.cloned.1.call-update
  69.1 0.0 copy-done.3
  69.1 0.7 broadcast_in_dim.33
  69.7 4.5 %all-to-all-start = ((s32[32,2,512]{2,1,0:T(2,128)}), s32[32,2,512]{2,1,0:T(2,128)S(1)}, u32[]{:S(2)}, u32[]{:S(2)}) async-start(s32[32,2,512]{2,1,0:T(2,128)} %broadcast_in_dim.33), calls=%async_computation | async-start | bytes 262144 | tf_op jit(solution)/shard_map/all_to_all | solution.py:21
  74.3 0.0 copy-done.2
  74.3 9.2 %gather_fusion = bf16[2048,512]{1,0:T(8,128)(2,1)} fusion(bf16[2048,512]{1,0:T(8,128)(2,1)S(1)} %select_bitcast_fusion, s32[2048]{0:T(1024)S(1)} %fusion.19), kind=kCustom, calls=%fused_computation | custom fusion | bytes 4202496 | tf_op jit(solution)/shard_map/jit(_take)/gather | solution.py:110
  83.5 3.4 all-to-all-done
  87.0 0.1 fusion.22
  87.1 137.8 %all-gather.2.cloned.1.call-done = bf16[16384,16,8]{0,1,2:T(8,128)(2,1)} async-done(((bf16[512,16,8]{0,1,2:T(8,128)(2,1)}), bf16[16384,16,8]{0,1,2:T(8,128)(2,1)}) %all-gather.2.cloned.1.call-update) | async-done | bytes 4194320 | tf_op jit(solution)/shard_map/all_gather | solution.py:97
  224.9 0.0 copy-start.1
  224.9 22.9 %fusion.9 = bf16[512,16,8]{0,1,2:T(8,128)(2,1)S(1)} fusion(bf16[16384,16,8]{0,1,2:T(8,128)(2,1)} %all-gather.2.cloned.1.call-done, s32[16384]{0:T(1024)S(1)} %bitcast.53, s32[512]{0:T(512)S(1)} %bitcast.55, s32[16384]{0:T(1024)S(1)} %bitcast.52, s32[512]{0:T(512)S(1)} %bitcast.54), kind=kOutput, calls=%fused_computation.12 | convolution fusion | flops 2239823872 | bytes 4460544 | tf_op jit(solution)/shard_map/dot_general | solution.py:99
  247.8 0.7 copy.21
  248.6 6.0 %all-to-all-start.3 = ((bf16[512,16,8]{0,2,1:T(8,128)(2,1)}), bf16[512,16,8]{0,2,1:T(8,128)(2,1)S(1)}, u32[]{:S(2)}, u32[]{:S(2)}) async-start(bf16[512,16,8]{0,2,1:T(8,128)(2,1)} %copy.21), calls=%async_computation.3 | async-start | bytes 262144 | tf_op jit(solution)/shard_map/all_to_all | solution.py:102
  254.5 0.0 reduce-scatter.5.cloned.1.call-start
  254.6 0.0 copy-done.1
  254.6 1.6 broadcast_select_fusion
  256.1 2.5 select_n.30
  258.7 4.6 %all-to-all-done.3 = bf16[512,16,8]{0,2,1:T(8,128)(2,1)S(1)} async-done(((bf16[512,16,8]{0,2,1:T(8,128)(2,1)}), bf16[512,16,8]{0,2,1:T(8,128)(2,1)S(1)}, u32[]{:S(2)}, u32[]{:S(2)}) %all-to-all-start.3) | async-done | bytes 131104 | tf_op jit(solution)/shard_map/all_to_all | solution.py:102
  263.3 1.3 fusion.6
  264.6 1.1 copy.24
  265.7 0.0 reduce-scatter.5.cloned.1.call-update
  265.8 0.0 reduce-scatter.7.cloned.1.call-start
  265.8 32.9 %reduce-scatter.5.cloned.1.call-done = f32[128,4,128]{2,0,1:T(8,128)} async-done(((f32[512,4,128]{2,0,1:T(8,128)}), f32[128,4,128]{2,0,1:T(8,128)}) %reduce-scatter.5.cloned.1.call-update) | async-done | bytes 262160 | tf_op jit(solution)/shard_map/reduce_scatter | solution.py:46
  298.7 0.0 reduce-scatter.7.cloned.1.call-update
  298.7 0.0 reduce-scatter.9.cloned.1.call-start
  298.8 26.7 %reduce-scatter.7.cloned.1.call-done = f32[32,4,128]{2,0,1:T(8,128)} async-done(((f32[128,4,128]{2,0,1:T(8,128)}), f32[32,4,128]{2,0,1:T(8,128)}) %reduce-scatter.7.cloned.1.call-update) | async-done | bytes 65552 | tf_op jit(solution)/shard_map/reduce_scatter | solution.py:46
  325.4 0.0 reduce-scatter.9.cloned.1.call-update
  325.5 0.0 reduce-scatter.11.cloned.1.call-start
  325.5 26.2 %reduce-scatter.9.cloned.1.call-done = f32[16,4,128]{2,0,1:T(8,128)} async-done(((f32[32,4,128]{2,0,1:T(8,128)}), f32[16,4,128]{2,0,1:T(8,128)}) %reduce-scatter.9.cloned.1.call-update) | async-done | bytes 32784 | tf_op jit(solution)/shard_map/reduce_scatter | solution.py:46
  351.7 0.0 reduce-scatter.11.cloned.1.call-update
  351.7 1.3 dynamic-slice
  353.0 13.0 %reduce-scatter.11.cloned.1.call-done = f32[8,4,128]{2,0,1:T(8,128)} async-done(((f32[16,4,128]{2,0,1:T(8,128)}), f32[8,4,128]{2,0,1:T(8,128)}) %reduce-scatter.11.cloned.1.call-update) | async-done | bytes 16400 | tf_op jit(solution)/shard_map/reduce_scatter | solution.py:46
  366.0 0.7 copy.25
  366.7 29.7 %all-reduce = f32[8,4,128]{2,1,0:T(4,128)S(1)} all-reduce(f32[8,4,128]{2,1,0:T(4,128)S(1)} %copy.25), channel_id=6, replica_groups=mesh['tm_0'=4,'tm_1'=2,'tm_2'=2,'cell_0'=8,'cell_1'=4] {'cell_0'}, use_global_device_ids=true, to_apply=%region_4.5.clone | all-reduce | flops 4096 | bytes 32768
  396.4 1.2 dynamic-slice_bitcast_fusion
  (4 shorter events, 0.0 us)
Async XLA Ops:
  6.5 61.6 %copy-start = (f32[16,16]{1,0:T(8,128)S(1)}, f32[16,16]{1,0:T(8,128)}, u32[]{:S(2)}) copy-start(f32[16,16]{1,0:T(8,128)} %param.8) | copy-start | bytes 3076
  8.2 42.9 %all-to-all-start.1 = ((bf16[512,4,128]{2,1,0:T(4,128)(2,1)}), bf16[512,4,128]{2,1,0:T(4,128)(2,1)S(1)}, u32[]{:S(2)}, u32[]{:S(2)}) async-start(bf16[512,4,128]{2,1,0:T(4,128)(2,1)} %stack.2), calls=%async_computation.1 | async-start | bytes 1048576 | tf_op jit(solution)/shard_map/all_to_all | solution.py:84
  29.4 195.5 %all-gather.2.cloned.1.call-start = ((), (), s32[]{:S(2)}) async-start(), calls=%async_computation.8 | async-start | bytes 4325376 | tf_op jit(solution)/shard_map/all_gather | solution.py:97
  30.1 38.9 %copy-start.3 = (s32[2,512]{1,0:T(2,128)S(1)}, s32[2,512]{1,0:T(2,128)}, u32[]{:S(2)}) copy-start(s32[2,512]{1,0:T(2,128)} %param.9) | copy-start | bytes 12292
  30.1 44.2 %copy-start.2 = (s32[2048]{0:T(1024)S(1)}, s32[2048]{0:T(1024)}, u32[]{:S(2)}) copy-start(s32[2048]{0:T(1024)} %param.11) | copy-start | bytes 24580
  69.7 17.2 %all-to-all-start = ((s32[32,2,512]{2,1,0:T(2,128)}), s32[32,2,512]{2,1,0:T(2,128)S(1)}, u32[]{:S(2)}, u32[]{:S(2)}) async-start(s32[32,2,512]{2,1,0:T(2,128)} %broadcast_in_dim.33), calls=%async_computation | async-start | bytes 262144 | tf_op jit(solution)/shard_map/all_to_all | solution.py:21
  224.9 29.7 %copy-start.1 = (bf16[2048,512]{1,0:T(8,128)(2,1)S(1)}, bf16[2048,512]{1,0:T(8,128)(2,1)}, u32[]{:S(2)}) copy-start(bf16[2048,512]{1,0:T(8,128)(2,1)} %gather_fusion) | copy-start | bytes 6291460
  248.6 14.8 %all-to-all-start.3 = ((bf16[512,16,8]{0,2,1:T(8,128)(2,1)}), bf16[512,16,8]{0,2,1:T(8,128)(2,1)S(1)}, u32[]{:S(2)}, u32[]{:S(2)}) async-start(bf16[512,16,8]{0,2,1:T(8,128)(2,1)} %copy.21), calls=%async_computation.3 | async-start | bytes 262144 | tf_op jit(solution)/shard_map/all_to_all | solution.py:102
  254.5 44.2 %reduce-scatter.5.cloned.1.call-start = ((), (), s32[]{:S(2)}) async-start(), calls=%async_computation.9 | async-start | bytes 1310720 | tf_op jit(solution)/shard_map/reduce_scatter | solution.py:46
  265.8 59.7 %reduce-scatter.7.cloned.1.call-start = ((), (), s32[]{:S(2)}) async-start(), calls=%async_computation.10 | async-start | bytes 327680 | tf_op jit(solution)/shard_map/reduce_scatter | solution.py:46
  298.7 53.0 %reduce-scatter.9.cloned.1.call-start = ((), (), s32[]{:S(2)}) async-start(), calls=%async_computation.11 | async-start | bytes 98304 | tf_op jit(solution)/shard_map/reduce_scatter | solution.py:46
  325.5 40.5 %reduce-scatter.11.cloned.1.call-start = ((), (), s32[]{:S(2)}) async-start(), calls=%async_computation.12 | async-start | bytes 49152 | tf_op jit(solution)/shard_map/reduce_scatter | solution.py:46
Sparse Core Ops, SparseCore 0:
  69.2 155.6 all-gather.1
  265.9 32.7 reduce-scatter.4
  301.7 23.6 reduce-scatter.6
  328.0 23.6 reduce-scatter.8
  354.3 11.6 reduce-scatter.10
